TPU v7x, 32 devices: a whole 2x2x4 slice. The times are simulated.
32 devices in a mesh: prow: 8 (over y, x, core), pcol: 4 (over z).
Axes of the slice: x: 2, y: 2, z: 4, core: 2. Of those that a mesh axis runs over, the one named last changes fastest.
Arguments:
- packed: bfloat16 [6144, 6144], P('prow', 'pcol'), may hold values from -32 to 32, as said below
- tile_scales: float32 [24, 24], P('prow', 'pcol'), may hold values from 0.5 to 2
Outputs:
- factored: bfloat16 [6144, 6144], P('prow', 'pcol')
Inputs may be any that keep to these rules, and one draw needn't show every extreme that they name: `packed`: stored tile entries lie in the range below.
All inputs are finite; a program needn't handle non-finite values.
Results may differ from a plain program's by a relative error of at most 0.0065.
Values may be sent and summed in bfloat16 or wider, within the bound.
No kernel may reach another device: no remote copies, remote signals or barrier semaphores. Data moves between devices by JAX's collectives and lax.ppermute only.
A program may use at most 64 MiB of HBM per device.

v0:
```python
import functools

import jax
import jax.numpy as jnp
import numpy as np
from jax import lax
from jax.experimental import pallas as pl
from jax.experimental.pallas import tpu as pltpu
from jax.sharding import PartitionSpec as P

F32 = jnp.float32
BF16 = jnp.bfloat16
HALF = 128
EXTRA = 16


def dot_nt(a, b, precision=None):
    dims = (((1,), (1,)), ((), ()))
    return lax.dot_general(a, b, dims, precision=precision, preferred_element_type=F32)


def dot_nn(a, b, precision=None):
    dims = (((1,), (0,)), ((), ()))
    return lax.dot_general(a, b, dims, precision=precision, preferred_element_type=F32)


HIGHEST = lax.Precision.HIGHEST


def inverse_factor(a):
    n = a.shape[0]
    blocks = n // 8
    full = (8, n)
    rows = [a[8 * i : 8 * i + 8, :] for i in range(blocks)]
    lane = lax.broadcasted_iota(jnp.int32, full, 1)
    sub = lax.broadcasted_iota(jnp.int32, full, 0)

    def column(x, k):
        return jnp.broadcast_to(x[:, k : k + 1], full)

    def row(x, k):
        return jnp.broadcast_to(x[k : k + 1, :], full)

    out = []
    own = [column(rows[0], k) for k in range(8)]
    for t in range(blocks):
        base = 8 * t
        here = jnp.logical_and(lane >= base, lane < base + 8)
        s = {(j, k): row(own[k], j) for j in range(8) for k in range(j, 8)}
        c = {}
        for i in range(t + 1, blocks):
            for j in range(8):
                c[i, j] = column(rows[i], base + j)
        last = t + 1 == blocks
        if not last:
            own = [column(rows[t + 1], base + 8 + k) for k in range(8)]
        for i in range(t + 1, blocks):
            rows[i] = jnp.where(here, 0.0, rows[i])
        b = [jnp.where(here, jnp.where(lane == base + j, 1.0, 0.0), row(rows[t], j)) for j in range(8)]
        d = [] if last else [c[t + 1, j] for j in range(8)]
        m = {}
        z = []
        x = jnp.zeros(full, F32)
        for j in range(8):
            r0 = pl.reciprocal(s[j, j], approx=True)
            e = 2.0 - s[j, j] * r0
            r = r0 * e
            for k in range(j + 1, 8):
                m[j, k] = s[j, k] * r
            for k in range(j + 1, 8):
                for l in range(k, 8):
                    if k == j + 1 and l == k:
                        s[k, l] = s[k, l] - ((s[j, k] * s[j, k]) * r0) * e
                    else:
                        s[k, l] = s[k, l] - m[j, k] * s[j, l]
                b[k] = b[k] - m[j, k] * b[j]
            z.append(r * b[j])
            if not last:
                for k in range(j + 1, 8):
                    d[k] = d[k] - m[j, k] * d[j]
                w = d[j] * r
                own = [own[k] - w * row(d[j], k) for k in range(8)]
                rows[t + 1] = rows[t + 1] - d[j] * z[j]
            x = jnp.where(sub == j, lax.rsqrt(s[j, j]) * b[j], x)
        out.append(jnp.where(lane < base + 8, x, 0.0))
        if t + 2 < blocks:
            y = list(z)
            for k in range(7, 0, -1):
                for j in range(k):
                    y[j] = y[j] - m[j, k] * y[k]
            for i in range(t + 2, blocks):
                for j in range(8):
                    rows[i] = rows[i] - c[i, j] * y[j]
    return jnp.concatenate(out, axis=0)


def split(x):
    high = x.astype(BF16)
    return high, (x - high.astype(F32)).astype(BF16)


def scale_row(ref, tile, n):
    tail = ref[n:, :].astype(F32)
    return tail[3 * tile : 3 * tile + 1] + tail[3 * tile + 1 : 3 * tile + 2] + tail[3 * tile + 2 : 3 * tile + 3]


def first_half(tile, inv_ref, low_ref, rest_ref):
    x = inverse_factor(tile[:HALF, :HALF])
    factor = dot_nt(tile[HALF:, :HALF], x, HIGHEST)
    inv_ref[...] = x
    low_ref[...] = factor
    rest_ref[...] = tile[HALF:, HALF:] - dot_nt(factor, factor, HIGHEST)


def second_half(inv_ref, low_ref, rest_ref, out_ref):
    x22 = inverse_factor(rest_ref[...])
    x11 = inv_ref[...]
    x21 = -dot_nn(x22, dot_nn(low_ref[...], x11, HIGHEST), HIGHEST)
    for k, x in enumerate((x11, x21, x22)):
        out_ref[k], out_ref[k + 3] = split(x)


def scale_tail(scales, n):
    row = lax.broadcasted_iota(jnp.int32, (EXTRA, n), 0)
    total = jnp.zeros((EXTRA, n), F32)
    for t in range(scales.shape[0]):
        rest = jnp.full((EXTRA, n), scales[t, 0], F32)
        for k in range(3):
            part = rest.astype(BF16).astype(F32)
            total = jnp.where(row == 3 * t + k, part, total)
            rest = rest - part
    return total.astype(BF16)


def pack_kernel(scales, packed, message, pivot, sem):
    n = pivot.shape[1]
    tall = message.shape[0] - EXTRA
    tile_copy = pltpu.make_async_copy(packed.at[0:n, 0:n], pivot.at[0:n], sem.at[0])
    block_copy = pltpu.make_async_copy(packed.at[:, 0:n], message.at[0:tall], sem.at[1])
    tile_copy.start()
    block_copy.start()
    tail = scale_tail(scales, n)
    pivot[n:, :] = tail
    message[tall:, :] = tail
    tile_copy.wait()
    block_copy.wait()


def take(tiles, mask, target):
    for k, tile in enumerate(tiles):

        @pl.when(mask == 2 * k)
        def _(tile=tile):
            n = target.shape[0]
            target[...] = tile[:n, :].astype(F32) * scale_row(tile, 0, n)


def factor_kernel(*refs):
    tiles, out_ref, left, tile, inv, low, rest = refs[:-6], *refs[-6:]
    n = 2 * HALF
    r = lax.axis_index("prow")
    place = r - r % 2

    @pl.when(r % 2 != lax.axis_index("pcol") % 2)
    def _():
        take(tiles, place, tile)
        take(tiles, place ^ 2, left)
        first_half(tile, inv, low, rest)
        second_half(inv, low, rest, out_ref.at[0:6])
        take(tiles, place ^ 4, tile)
        high, part = split(left[...])
        cat = join(out_ref, 0)
        both = jnp.concatenate([cat[:, :n], cat[:, :n], cat[:, n:]], axis=1)
        panel = dot_nt(jnp.concatenate([high, part, high], axis=1), both).astype(BF16)
        for k in range(4):
            i, j = divmod(k, 2)
            out_ref[12 + k] = panel[i * HALF : (i + 1) * HALF, j * HALF : (j + 1) * HALF]
        tile[...] = tile[...] - dot_nt(panel, panel)
        first_half(tile, inv, low, rest)
        second_half(inv, low, rest, out_ref.at[6:12])


def join(x, base):
    zero = jnp.zeros((HALF, HALF), BF16)
    upper = jnp.concatenate([x[base], zero, x[base + 3], zero], axis=1)
    lower = jnp.concatenate([x[base + 1], x[base + 2], x[base + 4], x[base + 5]], axis=1)
    return jnp.concatenate([upper, lower], axis=0)


VMEM = pl.BlockSpec(memory_space=pltpu.VMEM)
SMEM = pl.BlockSpec(memory_space=pltpu.SMEM)
HBM = pl.BlockSpec(memory_space=pltpu.HBM)
BLOCK = jax.ShapeDtypeStruct((HALF, HALF), F32)
PARTS = jax.ShapeDtypeStruct((6, HALF, HALF), BF16)
FACTORS = jax.ShapeDtypeStruct((16, HALF, HALF), BF16)


def factor_call(kernel, name, outs, args, specs=None, scratch=(), work=1):
    return pl.pallas_call(
        kernel,
        out_shape=outs,
        in_specs=specs or [VMEM] * len(args),
        out_specs=(VMEM,) * len(outs),
        scratch_shapes=scratch,
        compiler_params=pltpu.CompilerParams(vmem_limit_bytes=24 << 20),
        cost_estimate=pl.CostEstimate(flops=work * 5_000_000_000, bytes_accessed=0, transcendentals=0),
        name=name,
    )(*args)


def update_kernel(geometry, scales, packed, factors, factors_other, *rest):
    ratio, nr, nc, tpr, tpc, n = geometry
    here, there, mine, relayed = rest[0:2], rest[2:4], rest[4], rest[5]
    out, stored, result, block, rowp, colp, rowl, xs, sem = rest[6:]
    r = lax.axis_index("prow")
    c = lax.axis_index("pcol")
    tall = tpr * n

    reads = [pltpu.make_async_copy(packed.at[t * n : (t + 1) * n], stored.at[t], sem.at[0, t]) for t in range(tpr)]
    writes = [pltpu.make_async_copy(result.at[t], out.at[t * n : (t + 1) * n], sem.at[1, t]) for t in range(tpr)]
    for copy in reads:
        copy.start()

    def when(condition, target, value):
        @pl.when(condition)
        def _():
            target[...] = value[...]

    same = (r % 2) == (c % 2)
    when(jnp.logical_not(same), xs, factors)
    when(same, xs, factors_other)
    cat0 = join(xs, 0).T
    cat1 = join(xs, 6).T
    cat1 = jnp.concatenate([cat1[:n], cat1[:n], cat1[n:]], axis=0)
    panel = jnp.concatenate(
        [jnp.concatenate([xs[12], xs[13]], axis=1), jnp.concatenate([xs[14], xs[15]], axis=1)], axis=0
    ).T

    def solve(each):
        for t in range(tpr):
            rows = slice(t * n, (t + 1) * n)
            a0 = block[0, rows, :]
            raw0 = dot_nn(jnp.concatenate([a0, a0], axis=1), cat0)
            p0 = (raw0 * scale_row(block[0], t, tall)).astype(BF16)
            s1 = scale_row(block[1], t, tall)
            left = block[1, rows, :].astype(F32) * s1 - dot_nn(p0, panel)
            high, low = split(left)
            f1 = dot_nn(jnp.concatenate([high, low, high], axis=1), cat1)
            each(t, raw0, f1, s1, p0, f1.astype(BF16))

    early = jnp.where(c < 2, 0, 1)
    swap = r // 4 if (nr, nc) == (8, 4) else 0
    for g in range(ratio):
        for slot in range(ratio):
            chosen = (swap ^ g) == slot
            for half, panel_index in enumerate((early, 1 - early)):
                when(jnp.logical_and(chosen, same), block.at[panel_index], here[slot].at[half])
                when(jnp.logical_and(chosen, jnp.logical_not(same)), block.at[panel_index], there[slot].at[half])

        def keep_column(t, raw0, f1, s1, p0, p1, g=g):
            colp[t * ratio + g, :n, :] = p0.T
            colp[t * ratio + g, n:, :] = p1.T

        solve(keep_column)

    late = jnp.logical_and(nc == 4, jnp.where(r % 2 == 1, c == 2, c == 3))
    when(late, block, relayed)
    when(jnp.logical_not(late), block, mine)

    def keep_row(t, raw0, f1, s1, p0, p1):
        rowp[t, :, :n] = p0
        rowp[t, :, n:] = p1

        @pl.when(c == 0)
        def _():
            rowl[t] = raw0

        @pl.when(c == 1)
        def _():
            rowl[t] = f1 / s1

    solve(keep_row)

    for t in range(tpr):
        reads[t].wait()
        true_row = t * nr + r
        for q in range(tpc):
            true_col = q * nc + c
            cols = slice(q * n, (q + 1) * n)

            @pl.when(true_row < true_col)
            def _():
                result[t, :, cols] = stored[t, :, cols]

            @pl.when(jnp.logical_and(true_row >= true_col, true_col >= 2))
            def _():
                change = dot_nn(rowp[t], colp[q])
                inverse = 1.0 / jnp.full((1, n), scales[t, q], F32)
                result[t, :, cols] = (stored[t, :, cols].astype(F32) - change * inverse).astype(BF16)

            if q * nc < 2:

                @pl.when(jnp.logical_and(true_row >= true_col, true_col < 2))
                def _():
                    row = lax.broadcasted_iota(jnp.int32, (n, n), 0)
                    col = lax.broadcasted_iota(jnp.int32, (n, n), 1)
                    keep = jnp.logical_or(row >= col, true_row != true_col)
                    result[t, :, cols] = jnp.where(keep, rowl[t], 0.0).astype(BF16)

        writes[t].start()
    for copy in writes:
        copy.wait()


def update(scales, packed, arrays, nr, nc, tpr, tpc, n):
    geometry = (nr // nc, nr, nc, tpr, tpc, n)
    tall = arrays[-1].shape[1]
    return pl.pallas_call(
        functools.partial(update_kernel, geometry),
        out_shape=jax.ShapeDtypeStruct(packed.shape, BF16),
        in_specs=[SMEM, HBM] + [VMEM] * len(arrays),
        out_specs=HBM,
        scratch_shapes=[
            pltpu.VMEM((tpr, n, tpc * n), BF16),
            pltpu.VMEM((tpr, n, tpc * n), BF16),
            pltpu.VMEM((2, tall, n), BF16),
            pltpu.VMEM((tpr, n, 2 * n), BF16),
            pltpu.VMEM((tpc, 2 * n, n), BF16),
            pltpu.VMEM((tpr, n, n), F32),
            pltpu.VMEM(FACTORS.shape, BF16),
            pltpu.SemaphoreType.DMA((2, tpr)),
        ],
        compiler_params=pltpu.CompilerParams(vmem_limit_bytes=40 << 20),
        cost_estimate=pl.CostEstimate(flops=4_000_000_000, bytes_accessed=8 << 20, transcendentals=0),
        name="update_tiles",
    )(scales, packed, *arrays)


def on_device(nr, nc, packed, tile_scales):
    tpr, tpc = tile_scales.shape
    n = packed.shape[0] // tpr
    r = lax.axis_index("prow")
    c = lax.axis_index("pcol")
    def choose(options, index):
        value = options[0]
        for k in range(1, len(options)):
            value = jnp.where(index == k, options[k], value)
        return value

    def send(x, pairs):
        table = [(a * nc + b, d * nc + e) for (a, b), (d, e) in pairs]
        return lax.ppermute(x, ("prow", "pcol"), table)

    message, pivot = pl.pallas_call(
        pack_kernel,
        out_shape=(jax.ShapeDtypeStruct((tpr * n + EXTRA, n), BF16), jax.ShapeDtypeStruct((n + EXTRA, n), BF16)),
        in_specs=[SMEM, HBM],
        out_specs=(VMEM,) * 2,
        scratch_shapes=[pltpu.SemaphoreType.DMA((2,))],
        compiler_params=pltpu.CompilerParams(vmem_limit_bytes=48 << 20),
        name="pack_panel",
    )(tile_scales, pltpu.with_memory_space_constraint(packed, pltpu.HBM))

    other = [(k + 1) % 2 for k in range(nc)]
    came = []
    for k in range(nc):
        came.append(send(pivot, [((0, 0), (other[k], k)), ((1, 0), (2 + other[k], k)), ((1, 1), (4 + other[k], k))]))
    tile = choose(came, c)
    tiles = [tile]
    for mask in range(2, nr, 2):
        tiles.append(send(tile, [((a + other[e], e), ((a + other[e]) ^ mask, e)) for a in (0, 2, 4) for e in range(nc)]))
    scratch = [pltpu.VMEM((n, n), F32)] * 2 + [pltpu.VMEM((HALF, HALF), F32)] * 3
    (factors,) = factor_call(factor_kernel, "factor_pivots", (FACTORS,), tuple(tiles), None, scratch, 0)

    u = r % nc
    if nc == 4:
        first = {0: [(1, 0), (0, 2)], 1: [(0, 1), (1, 3)], 2: [(1, 2), (0, 1)], 3: [(1, 3), (0, 1)]}
        second = {0: [(1, 2), (0, 1)], 1: [(0, 3), (1, 0)], 2: [(0, 2), (1, 0)], 3: [(0, 3), (1, 0)]}
        turns = [[((a, x), (a, y)) for a in range(nr) for x, y in t[a % 4]] for t in (first, second)]
        got = [send(message, turn) for turn in turns]
    else:
        got = [jnp.zeros_like(message)] * 2
        for panel in range(2):
            for k in range(nc):
                if k != panel:
                    came = send(message, [((a, panel), (a, k)) for a in range(nr)])
                    slot = panel if k == 0 else 1 - panel if k > 1 else 0
                    got[slot] = jnp.where(c == k, came, got[slot])
    factors, *got = lax.optimization_barrier((factors, *got))

    ratio = nr // nc

    parity = [(a, e) for a in range(nr) for e in range(nc) if a % 2 == e % 2]

    def spread(x):
        if (nr, nc) == (8, 4):
            got = send(x, [((e + 4 * g, e), ((e + 4 * g) ^ 2, e)) for e in range(nc) for g in range(2)])
            side = jnp.where(u == c, x, got)
            return [side, send(side, [((a, e), (a ^ 4, e)) for a, e in parity])]
        near = [x]
        for mask in range(2, nr, 2):
            pairs = [((e + nc * g, e), ((e + nc * g) ^ mask, e)) for e in range(nc) for g in range(ratio)]
            near.append(send(x, pairs))
        return [choose(near, (r ^ (c + nc * g)) // 2) for g in range(ratio)]

    early = spread(jnp.where(c == 0, message, got[0]))
    late = spread(jnp.where(c == 0, got[0], jnp.where(c == 1, message, got[1])))
    if nc == 4:
        swap = (u == 0) == (c >= 2)
        m0 = jnp.where(c == 0, message, jnp.where(swap, got[0], got[1]))
        m0 = jnp.where(c == 1, jnp.where(u == 0, got[1], got[0]), m0)
        m1 = jnp.where(c == 1, message, jnp.where(swap, got[1], got[0]))
        m1 = jnp.where(c == 0, jnp.where(u == 0, got[0], got[1]), m1)
        mine = jnp.stack([m0, m1])
        relayed = send(mine, [((a, 3), (a, 2)) if a % 2 else ((a, 2), (a, 3)) for a in range(nr)])
    else:
        m0 = jnp.where(c == 0, message, jnp.where(c == 1, got[0], got[1]))
        mine = jnp.stack([m0, jnp.where(c == 1, message, got[0])])
        relayed = mine

    cols = [jnp.stack([early[g], late[g]]) for g in range(ratio)]
    cols_other = [send(x, [((a, e), (a ^ 1, e)) for a, e in parity]) for x in cols]
    factors_other = send(factors, [((a ^ 1, e), (a, e)) for a, e in parity])
    packed = pltpu.with_memory_space_constraint(packed, pltpu.HBM)
    arrays = (factors, factors_other, *cols, *cols_other, mine, relayed)
    return update(tile_scales, packed, arrays, nr, nc, tpr, tpc, n)


def solution(mesh):
    nr = mesh.shape["prow"]
    nc = mesh.shape["pcol"]
    return jax.shard_map(
        functools.partial(on_device, nr, nc),
        mesh=mesh,
        in_specs=(P("prow", "pcol"), P("prow", "pcol")),
        out_specs=P("prow", "pcol"),
        check_vma=False,
    )
```

profile of v0, /device:TPU:24, one launch (start us, length us, event | category | flops | bytes accessed | tf_op | source)
XLA Modules:
  0.0 75.1 jit_solution(14521322604259476668)
XLA Ops:
  0.0 0.0 copy-start
  0.0 0.7 copy-done
  0.7 1.7 %pack_panel.1 = (bf16[784,256]{1,0:T(8,128)(2,1)S(1)}, bf16[272,256]{1,0:T(8,128)(2,1)S(1)}) custom-call(f32[3,6]{1,0:T(4,128)S(1)} %copy-done, bf16[768,1536]{1,0:T(8,128)(2,1)} %packed.3), custom_call_target="tpu_custom_call" | custom-call | tf_op jit(solution)/shard_map/pack_panel/pallas_call | solution.py:354
  2.4 0.7 collective-permute-start.3
  3.0 0.7 collective-permute-start.2
  3.7 0.7 collective-permute-start.1
  4.4 1.3 %collective-permute-start = (bf16[272,256]{1,0:T(8,128)(2,1)S(1)}, bf16[272,256]{1,0:T(8,128)(2,1)S(1)}, u32[]{:S(2)}, u32[]{:S(2)}) collective-permute-start(bf16[272,256]{1,0:T(8,128)(2,1)S(1)} %get-tuple-element.10), channel_id=1, source_target_pairs={{0,3},{4,11},{5,19}} | collective-permute-start | bytes 417800 | tf_op jit(solution)/shard_map/ppermute | solution.py:352
  5.7 0.7 collective-permute-start.8
  6.4 0.0 collective-permute-done.3
  6.4 0.7 collective-permute-start.7
  7.1 0.0 collective-permute-done.2
  7.1 0.0 collective-permute-done.1
  7.1 9.9 %collective-permute-done = bf16[272,256]{1,0:T(8,128)(2,1)S(1)} collective-permute-done((bf16[272,256]{1,0:T(8,128)(2,1)S(1)}, bf16[272,256]{1,0:T(8,128)(2,1)S(1)}, u32[]{:S(2)}, u32[]{:S(2)}) %collective-permute-start) | collective-permute-done | bytes 139296 | tf_op jit(solution)/shard_map/ppermute | solution.py:352
  17.1 1.3 %collective-permute-start.6 = (bf16[272,256]{1,0:T(8,128)(2,1)S(1)}, bf16[272,256]{1,0:T(8,128)(2,1)S(1)}, u32[]{:S(2)}, u32[]{:S(2)}) collective-permute-start(bf16[272,256]{1,0:T(8,128)(2,1)S(1)} %select_select_fusion.1.refs_0_), channel_id=1, source_target_pairs={{4,28},{1,25},{6,30},{3,27},{12,20},{9,17},{14,22},{11,19},{20,12}... | collective-permute-start | bytes 417800 | tf_op jit(solution)/shard_map/ppermute | solution.py:352
  18.4 9.3 %collective-permute-start.5 = (bf16[272,256]{1,0:T(8,128)(2,1)S(1)}, bf16[272,256]{1,0:T(8,128)(2,1)S(1)}, u32[]{:S(2)}, u32[]{:S(2)}) collective-permute-start(bf16[272,256]{1,0:T(8,128)(2,1)S(1)} %select_select_fusion.1.refs_0_), channel_id=1, source_target_pairs={{4,20},{1,17},{6,22},{3,19},{12,28},{9,25},{14,30},{11,27},{20,4},... | collective-permute-start | bytes 417800 | tf_op jit(solution)/shard_map/ppermute | solution.py:352
  27.7 2.7 %collective-permute-start.4 = (bf16[272,256]{1,0:T(8,128)(2,1)S(1)}, bf16[272,256]{1,0:T(8,128)(2,1)S(1)}, u32[]{:S(2)}, u32[]{:S(2)}) collective-permute-start(bf16[272,256]{1,0:T(8,128)(2,1)S(1)} %select_select_fusion.1.refs_0_), channel_id=1, source_target_pairs={{4,12},{1,9},{6,14},{3,11},{12,4},{9,1},{14,6},{11,3},{20,28},{17,... | collective-permute-start | bytes 417800 | tf_op jit(solution)/shard_map/ppermute | solution.py:352
  30.5 0.0 collective-permute-done.6.refs_3_
  30.5 0.2 collective-permute-done.5.refs_2_
  30.8 3.9 %collective-permute-done.4.refs_1_ = bf16[272,256]{1,0:T(8,128)(2,1)S(1)} collective-permute-done((bf16[272,256]{1,0:T(8,128)(2,1)S(1)}, bf16[272,256]{1,0:T(8,128)(2,1)S(1)}, u32[]{:S(2)}, u32[]{:S(2)}) %collective-permute-start.4) | collective-permute-done | bytes 139296 | tf_op jit(solution)/shard_map/ppermute | solution.py:352
  34.7 14.9 %factor_pivots.1.factors = bf16[16,128,128]{2,1,0:T(8,128)(2,1)S(1)} custom-call(bf16[272,256]{1,0:T(8,128)(2,1)S(1)} %select_select_fusion.1.refs_0_, bf16[272,256]{1,0:T(8,128)(2,1)S(1)} %collective-permute-done.4.refs_1_, bf16[272,256]{1,0:T(8,128)(2,1)S(1)} %collective-permute-done.5.refs_2_, bf16[272,256]{1,0:T(8,128)(2,1)S(1)} %collective-permute-done.6.refs_3_), custom_call_target="tpu_custom_call" | custom-call | tf_op jit(solution)/shard_map/factor_pivots/pallas_call | solution.py:199
  49.6 0.0 collective-permute-done.8
  49.6 0.0 collective-permute-done.7
  49.6 0.2 select_bitcast_fusion.1
  49.8 0.7 collective-permute-start.11
  50.5 0.7 collective-permute-start.10
  51.2 0.0 collective-permute-done.11
  51.3 0.7 collective-permute-start.13
  52.0 0.0 collective-permute-done.10
  52.0 0.7 collective-permute-start.12
  52.7 0.0 copy-start.1
  52.7 0.1 pad_maximum_fusion.2.rest_4_
  52.8 1.3 %collective-permute-start.16 = (bf16[2,784,256]{2,1,0:T(8,128)(2,1)S(1)}, bf16[2,784,256]{2,1,0:T(8,128)(2,1)S(1)}, u32[]{:S(2)}, u32[]{:S(2)}) collective-permute-start(bf16[2,784,256]{2,1,0:T(8,128)(2,1)S(1)} %pad_maximum_fusion.2.rest_4_), channel_id=1, source_target_pairs={{2,3},{7,6},{10,11},{15,14},{18,19},{23,22},{26,27},{31,30}} | collective-permute-start | bytes 2408456 | tf_op jit(solution)/shard_map/ppermute | solution.py:352
  54.1 0.1 pad_maximum_fusion.rest_0_
  54.2 1.3 %collective-permute-start.14 = (bf16[2,784,256]{2,1,0:T(8,128)(2,1)S(1)}, bf16[2,784,256]{2,1,0:T(8,128)(2,1)S(1)}, u32[]{:S(2)}, u32[]{:S(2)}) collective-permute-start(bf16[2,784,256]{2,1,0:T(8,128)(2,1)S(1)} %pad_maximum_fusion.rest_0_), channel_id=1, source_target_pairs={{0,4},{2,6},{5,1},{7,3},{8,12},{10,14},{13,9},{15,11},{16,20},{18,... | collective-permute-start | bytes 2408456 | tf_op jit(solution)/shard_map/ppermute | solution.py:352
  55.5 0.0 collective-permute-done.13
  55.5 0.0 collective-permute-done.12
  55.5 0.1 pad_maximum_fusion.1.rest_1_
  55.6 1.3 %collective-permute-start.15 = (bf16[2,784,256]{2,1,0:T(8,128)(2,1)S(1)}, bf16[2,784,256]{2,1,0:T(8,128)(2,1)S(1)}, u32[]{:S(2)}, u32[]{:S(2)}) collective-permute-start(bf16[2,784,256]{2,1,0:T(8,128)(2,1)S(1)} %pad_maximum_fusion.1.rest_1_), channel_id=1, source_target_pairs={{0,4},{2,6},{5,1},{7,3},{8,12},{10,14},{13,9},{15,11},{16,20},{18,... | collective-permute-start | bytes 2408456 | tf_op jit(solution)/shard_map/ppermute | solution.py:352
  56.9 3.2 %collective-permute-start.9 = (bf16[16,128,128]{2,1,0:T(8,128)(2,1)S(1)}, bf16[16,128,128]{2,1,0:T(8,128)(2,1)S(1)}, u32[]{:S(2)}, u32[]{:S(2)}) collective-permute-start(bf16[16,128,128]{2,1,0:T(8,128)(2,1)S(1)} %factor_pivots.1.factors), channel_id=1, source_target_pairs={{4,0},{6,2},{1,5},{3,7},{12,8},{14,10},{9,13},{11,15},{20,16},{22,... | collective-permute-start | bytes 1572872 | tf_op jit(solution)/shard_map/ppermute | solution.py:352
  60.1 1.5 %collective-permute-done.9.factors_other = bf16[16,128,128]{2,1,0:T(8,128)(2,1)S(1)} collective-permute-done((bf16[16,128,128]{2,1,0:T(8,128)(2,1)S(1)}, bf16[16,128,128]{2,1,0:T(8,128)(2,1)S(1)}, u32[]{:S(2)}, u32[]{:S(2)}) %collective-permute-start.9) | collective-permute-done | bytes 524320 | tf_op jit(solution)/shard_map/ppermute | solution.py:352
  61.6 5.3 %collective-permute-done.16.rest_5_ = bf16[2,784,256]{2,1,0:T(8,128)(2,1)S(1)} collective-permute-done((bf16[2,784,256]{2,1,0:T(8,128)(2,1)S(1)}, bf16[2,784,256]{2,1,0:T(8,128)(2,1)S(1)}, u32[]{:S(2)}, u32[]{:S(2)}) %collective-permute-start.16) | collective-permute-done | bytes 802848 | tf_op jit(solution)/shard_map/ppermute | solution.py:352
  66.9 0.0 collective-permute-done.14.rest_2_
  66.9 0.0 collective-permute-done.15.rest_3_
  66.9 0.0 copy-done.1
  66.9 8.0 %update_tiles.1 = bf16[768,1536]{1,0:T(8,128)(2,1)} custom-call(f32[3,6]{1,0:T(4,128)S(1)} %copy-done.1, bf16[768,1536]{1,0:T(8,128)(2,1)} %packed.3, bf16[16,128,128]{2,1,0:T(8,128)(2,1)S(1)} %factor_pivots.1.factors, bf16[16,128,128]{2,1,0:T(8,128)(2,1)S(1)} %collective-permute-done.9.factors_other, bf16[2,784,256]{2,1,0:T(8,128)(2,1)S(1)} %pad_maximum_fusion.rest_0_, ...), custom_call_target="tpu_custom_call" | custom-call | flops 4000000000 | bytes 8388608 | tf_op jit(solution)/shard_map/update_tiles/pallas_call | solution.py:318
  (3 shorter events, 0.1 us)
Async XLA Ops:
  0.0 0.7 copy-start
  2.4 4.0 %collective-permute-start.3 = (bf16[272,256]{1,0:T(8,128)(2,1)S(1)}, bf16[272,256]{1,0:T(8,128)(2,1)S(1)}, u32[]{:S(2)}, u32[]{:S(2)}) collective-permute-start(bf16[272,256]{1,0:T(8,128)(2,1)S(1)} %get-tuple-element.10), channel_id=1, source_target_pairs={{0,4},{4,12},{5,20}} | collective-permute-start | bytes 417800 | tf_op jit(solution)/shard_map/ppermute | solution.py:352
  3.0 4.1 %collective-permute-start.2 = (bf16[272,256]{1,0:T(8,128)(2,1)S(1)}, bf16[272,256]{1,0:T(8,128)(2,1)S(1)}, u32[]{:S(2)}, u32[]{:S(2)}) collective-permute-start(bf16[272,256]{1,0:T(8,128)(2,1)S(1)} %get-tuple-element.10), channel_id=1, source_target_pairs={{0,1},{4,9},{5,17}} | collective-permute-start | bytes 417800 | tf_op jit(solution)/shard_map/ppermute | solution.py:352
  3.7 3.4 %collective-permute-start.1 = (bf16[272,256]{1,0:T(8,128)(2,1)S(1)}, bf16[272,256]{1,0:T(8,128)(2,1)S(1)}, u32[]{:S(2)}, u32[]{:S(2)}) collective-permute-start(bf16[272,256]{1,0:T(8,128)(2,1)S(1)} %get-tuple-element.10), channel_id=1, source_target_pairs={{0,6},{4,14},{5,22}} | collective-permute-start | bytes 417800 | tf_op jit(solution)/shard_map/ppermute | solution.py:352
  4.4 12.7 %collective-permute-start = (bf16[272,256]{1,0:T(8,128)(2,1)S(1)}, bf16[272,256]{1,0:T(8,128)(2,1)S(1)}, u32[]{:S(2)}, u32[]{:S(2)}) collective-permute-start(bf16[272,256]{1,0:T(8,128)(2,1)S(1)} %get-tuple-element.10), channel_id=1, source_target_pairs={{0,3},{4,11},{5,19}} | collective-permute-start | bytes 417800 | tf_op jit(solution)/shard_map/ppermute | solution.py:352
  5.7 43.9 %collective-permute-start.8 = (bf16[784,256]{1,0:T(8,128)(2,1)S(1)}, bf16[784,256]{1,0:T(8,128)(2,1)S(1)}, u32[]{:S(2)}, u32[]{:S(2)}) collective-permute-start(bf16[784,256]{1,0:T(8,128)(2,1)S(1)} %get-tuple-element.11), channel_id=1, source_target_pairs={{1,2},{0,1},{4,7},{5,4},{8,10},{9,8},{12,15},{13,12},{17,18},{16,1... | collective-permute-start | bytes 1204232 | tf_op jit(solution)/shard_map/ppermute | solution.py:352
  6.4 43.2 %collective-permute-start.7 = (bf16[784,256]{1,0:T(8,128)(2,1)S(1)}, bf16[784,256]{1,0:T(8,128)(2,1)S(1)}, u32[]{:S(2)}, u32[]{:S(2)}) collective-permute-start(bf16[784,256]{1,0:T(8,128)(2,1)S(1)} %get-tuple-element.11), channel_id=1, source_target_pairs={{1,0},{0,2},{4,5},{5,7},{9,10},{8,9},{13,15},{12,13},{17,16},{16,1... | collective-permute-start | bytes 1204232 | tf_op jit(solution)/shard_map/ppermute | solution.py:352
  17.1 13.4 %collective-permute-start.6 = (bf16[272,256]{1,0:T(8,128)(2,1)S(1)}, bf16[272,256]{1,0:T(8,128)(2,1)S(1)}, u32[]{:S(2)}, u32[]{:S(2)}) collective-permute-start(bf16[272,256]{1,0:T(8,128)(2,1)S(1)} %select_select_fusion.1.refs_0_), channel_id=1, source_target_pairs={{4,28},{1,25},{6,30},{3,27},{12,20},{9,17},{14,22},{11,19},{20,12}... | collective-permute-start | bytes 417800 | tf_op jit(solution)/shard_map/ppermute | solution.py:352
  18.4 12.4 %collective-permute-start.5 = (bf16[272,256]{1,0:T(8,128)(2,1)S(1)}, bf16[272,256]{1,0:T(8,128)(2,1)S(1)}, u32[]{:S(2)}, u32[]{:S(2)}) collective-permute-start(bf16[272,256]{1,0:T(8,128)(2,1)S(1)} %select_select_fusion.1.refs_0_), channel_id=1, source_target_pairs={{4,20},{1,17},{6,22},{3,19},{12,28},{9,25},{14,30},{11,27},{20,4},... | collective-permute-start | bytes 417800 | tf_op jit(solution)/shard_map/ppermute | solution.py:352
  27.7 6.9 %collective-permute-start.4 = (bf16[272,256]{1,0:T(8,128)(2,1)S(1)}, bf16[272,256]{1,0:T(8,128)(2,1)S(1)}, u32[]{:S(2)}, u32[]{:S(2)}) collective-permute-start(bf16[272,256]{1,0:T(8,128)(2,1)S(1)} %select_select_fusion.1.refs_0_), channel_id=1, source_target_pairs={{4,12},{1,9},{6,14},{3,11},{12,4},{9,1},{14,6},{11,3},{20,28},{17,... | collective-permute-start | bytes 417800 | tf_op jit(solution)/shard_map/ppermute | solution.py:352
  49.8 1.4 %collective-permute-start.11 = (bf16[784,256]{1,0:T(8,128)(2,1)S(1)}, bf16[784,256]{1,0:T(8,128)(2,1)S(1)}, u32[]{:S(2)}, u32[]{:S(2)}) collective-permute-start(bf16[784,256]{1,0:T(8,128)(2,1)S(1)} %get-tuple-element.17), channel_id=1, source_target_pairs={{0,8},{16,24},{5,13},{21,29},{10,2},{26,18},{15,7},{31,23}} | collective-permute-start | bytes 1204232 | tf_op jit(solution)/shard_map/ppermute | solution.py:352
  50.5 1.5 %collective-permute-start.10 = (bf16[784,256]{1,0:T(8,128)(2,1)S(1)}, bf16[784,256]{1,0:T(8,128)(2,1)S(1)}, u32[]{:S(2)}, u32[]{:S(2)}) collective-permute-start(bf16[784,256]{1,0:T(8,128)(2,1)S(1)} %get-tuple-element.18), channel_id=1, source_target_pairs={{0,8},{16,24},{5,13},{21,29},{10,2},{26,18},{15,7},{31,23}} | collective-permute-start | bytes 1204232 | tf_op jit(solution)/shard_map/ppermute | solution.py:352
  51.3 4.2 %collective-permute-start.13 = (bf16[784,256]{1,0:T(8,128)(2,1)S(1)}, bf16[784,256]{1,0:T(8,128)(2,1)S(1)}, u32[]{:S(2)}, u32[]{:S(2)}) collective-permute-start(bf16[784,256]{1,0:T(8,128)(2,1)S(1)} %broadcast_select_fusion.1), channel_id=1, source_target_pairs={{0,16},{2,18},{5,21},{7,23},{8,24},{10,26},{13,29},{15,31},{16,0},... | collective-permute-start | bytes 1204232 | tf_op jit(solution)/shard_map/ppermute | solution.py:352
  52.0 3.5 %collective-permute-start.12 = (bf16[784,256]{1,0:T(8,128)(2,1)S(1)}, bf16[784,256]{1,0:T(8,128)(2,1)S(1)}, u32[]{:S(2)}, u32[]{:S(2)}) collective-permute-start(bf16[784,256]{1,0:T(8,128)(2,1)S(1)} %broadcast_select_fusion.2), channel_id=1, source_target_pairs={{0,16},{2,18},{5,21},{7,23},{8,24},{10,26},{13,29},{15,31},{16,0},... | collective-permute-start | bytes 1204232 | tf_op jit(solution)/shard_map/ppermute | solution.py:352
  52.7 14.2 %copy-start.1 = (f32[3,6]{1,0:T(4,128)S(1)}, f32[3,6]{1,0:T(4,128)}, u32[]{:S(2)}) copy-start(f32[3,6]{1,0:T(4,128)} %scales.3) | copy-start | bytes 220
  52.8 14.1 %collective-permute-start.16 = (bf16[2,784,256]{2,1,0:T(8,128)(2,1)S(1)}, bf16[2,784,256]{2,1,0:T(8,128)(2,1)S(1)}, u32[]{:S(2)}, u32[]{:S(2)}) collective-permute-start(bf16[2,784,256]{2,1,0:T(8,128)(2,1)S(1)} %pad_maximum_fusion.2.rest_4_), channel_id=1, source_target_pairs={{2,3},{7,6},{10,11},{15,14},{18,19},{23,22},{26,27},{31,30}} | collective-permute-start | bytes 2408456 | tf_op jit(solution)/shard_map/ppermute | solution.py:352
  54.2 12.7 %collective-permute-start.14 = (bf16[2,784,256]{2,1,0:T(8,128)(2,1)S(1)}, bf16[2,784,256]{2,1,0:T(8,128)(2,1)S(1)}, u32[]{:S(2)}, u32[]{:S(2)}) collective-permute-start(bf16[2,784,256]{2,1,0:T(8,128)(2,1)S(1)} %pad_maximum_fusion.rest_0_), channel_id=1, source_target_pairs={{0,4},{2,6},{5,1},{7,3},{8,12},{10,14},{13,9},{15,11},{16,20},{18,... | collective-permute-start | bytes 2408456 | tf_op jit(solution)/shard_map/ppermute | solution.py:352
  55.6 11.3 %collective-permute-start.15 = (bf16[2,784,256]{2,1,0:T(8,128)(2,1)S(1)}, bf16[2,784,256]{2,1,0:T(8,128)(2,1)S(1)}, u32[]{:S(2)}, u32[]{:S(2)}) collective-permute-start(bf16[2,784,256]{2,1,0:T(8,128)(2,1)S(1)} %pad_maximum_fusion.1.rest_1_), channel_id=1, source_target_pairs={{0,4},{2,6},{5,1},{7,3},{8,12},{10,14},{13,9},{15,11},{16,20},{18,... | collective-permute-start | bytes 2408456 | tf_op jit(solution)/shard_map/ppermute | solution.py:352
  56.9 4.7 %collective-permute-start.9 = (bf16[16,128,128]{2,1,0:T(8,128)(2,1)S(1)}, bf16[16,128,128]{2,1,0:T(8,128)(2,1)S(1)}, u32[]{:S(2)}, u32[]{:S(2)}) collective-permute-start(bf16[16,128,128]{2,1,0:T(8,128)(2,1)S(1)} %factor_pivots.1.factors), channel_id=1, source_target_pairs={{4,0},{6,2},{1,5},{3,7},{12,8},{14,10},{9,13},{11,15},{20,16},{22,... | collective-permute-start | bytes 1572872 | tf_op jit(solution)/shard_map/ppermute | solution.py:352
where the time goes:
time: 75.6 us; the launch traced here: 75.1 us
  starting transfers between devices  27.9 us (37%)
  Pallas kernels  24.6 us (33%)
  waiting for transfers between devices  20.9 us (28%)
    ppermute x17, starting transfers between devices, send(): return lax.ppermute(x, ('prow', 'pcol'), table)  27.9 us
    ppermute x17, waiting for transfers between devices, send(): return lax.ppermute(x, ('prow', 'pcol'), table)  20.9 us
    pallas_call x1, Pallas kernels, factor_call(): pl.pallas_call(kernel, out_shape=outs, in_specs=specs or [VMEM] * len(arg...  14.9 us
    pallas_call x1, Pallas kernels, update(): pl.pallas_call(functools.partial(update_kernel, geometry), out_shape=jax....  8.03 us
    pallas_call x1, Pallas kernels, on_device(): pl.pallas_call(pack_kernel, out_shape=(jax.ShapeDtypeStruct((tpr * n + EX...  1.66 us
  transfers between devices with their start and end apart: 17, of which 5 were waited for; matrix products, arithmetic and copies ran while one was open for 0% of the time, Pallas kernels for 20%

commit v1 on v0

--- a/solution.py
+++ b/solution.py
@@ -208,10 +208,10 @@
     )(*args)
 
 
-def update_kernel(geometry, scales, packed, factors, factors_other, *rest):
-    ratio, nr, nc, tpr, tpc, n = geometry
-    here, there, mine, relayed = rest[0:2], rest[2:4], rest[4], rest[5]
-    out, stored, result, block, rowp, colp, rowl, xs, sem = rest[6:]
+def update_kernel(geometry, table, scales, packed, factors, factors_other, *rest):
+    ratio, nr, nc, tpr, tpc, n, count = geometry
+    here, there, blocks = rest[0:2], rest[2:4], rest[4 : 4 + count]
+    out, stored, result, block, rowp, colp, rowl, xs, sem = rest[4 + count :]
     r = lax.axis_index("prow")
     c = lax.axis_index("pcol")
     tall = tpr * n
@@ -248,7 +248,7 @@
             f1 = dot_nn(jnp.concatenate([high, low, high], axis=1), cat1)
             each(t, raw0, f1, s1, p0, f1.astype(BF16))
 
-    early = jnp.where(c < 2, 0, 1)
+    early = jnp.where(c == 2, 1, 0) if nc == 4 else jnp.where(c < 2, 0, 1)
     swap = r // 4 if (nr, nc) == (8, 4) else 0
     for g in range(ratio):
         for slot in range(ratio):
@@ -263,9 +263,10 @@
 
         solve(keep_column)
 
-    late = jnp.logical_and(nc == 4, jnp.where(r % 2 == 1, c == 2, c == 3))
-    when(late, block, relayed)
-    when(jnp.logical_not(late), block, mine)
+    for panel_index in range(2):
+        index = table[2 * (r * nc + c) + panel_index]
+        for k in range(count):
+            when(index == k, block.at[panel_index], blocks[k])
 
     def keep_row(t, raw0, f1, s1, p0, p1):
         rowp[t, :, :n] = p0
@@ -312,13 +313,13 @@
         copy.wait()
 
 
-def update(scales, packed, arrays, nr, nc, tpr, tpc, n):
-    geometry = (nr // nc, nr, nc, tpr, tpc, n)
-    tall = arrays[-1].shape[1]
+def update(table, scales, packed, arrays, blocks, nr, nc, tpr, tpc, n):
+    geometry = (nr // nc, nr, nc, tpr, tpc, n, len(blocks))
+    tall = blocks[0].shape[0]
     return pl.pallas_call(
         functools.partial(update_kernel, geometry),
         out_shape=jax.ShapeDtypeStruct(packed.shape, BF16),
-        in_specs=[SMEM, HBM] + [VMEM] * len(arrays),
+        in_specs=[SMEM, SMEM, HBM] + [VMEM] * (len(arrays) + len(blocks)),
         out_specs=HBM,
         scratch_shapes=[
             pltpu.VMEM((tpr, n, tpc * n), BF16),
@@ -333,7 +334,7 @@
         compiler_params=pltpu.CompilerParams(vmem_limit_bytes=40 << 20),
         cost_estimate=pl.CostEstimate(flops=4_000_000_000, bytes_accessed=8 << 20, transcendentals=0),
         name="update_tiles",
-    )(scales, packed, *arrays)
+    )(table, scales, packed, *arrays, *blocks)
 
 
 def on_device(nr, nc, packed, tile_scales):
@@ -373,57 +374,71 @@
     (factors,) = factor_call(factor_kernel, "factor_pivots", (FACTORS,), tuple(tiles), None, scratch, 0)
 
     u = r % nc
+    blocks = [message]
+    holds = {(a, p, p): 0 for a in range(nr) for p in range(2)}
+
+    def send_round(operand, moves):
+        for a, b, d, k in moves:
+            holds[a, d, next(p for p in range(2) if holds.get((a, b, p)) == k)] = len(blocks)
+        blocks.append(send(operand, [((a, b), (a, d)) for a, b, d, _ in moves]))
+
     if nc == 4:
-        first = {0: [(1, 0), (0, 2)], 1: [(0, 1), (1, 3)], 2: [(1, 2), (0, 1)], 3: [(1, 3), (0, 1)]}
-        second = {0: [(1, 2), (0, 1)], 1: [(0, 3), (1, 0)], 2: [(0, 2), (1, 0)], 3: [(0, 3), (1, 0)]}
-        turns = [[((a, x), (a, y)) for a in range(nr) for x, y in t[a % 4]] for t in (first, second)]
-        got = [send(message, turn) for turn in turns]
+        first = {0: [(1, 0), (0, 2)], 1: [(0, 1), (1, 3)], 2: [(1, 2), (0, 1)], 3: [(0, 3), (1, 0)]}
+        second = {0: [(1, 2), (0, 1)], 1: [(0, 3), (1, 0)], 2: [(0, 2), (1, 0)], 3: [(1, 3), (0, 1)]}
+        light = ({0: [(1, 0)], 1: [(0, 1)]}, {0: [(0, 2), (1, 3)], 1: [(0, 3), (1, 2)]})
+        for turn, alone in zip((first, second), light):
+            send_round(message, [(a, *move, 0) for a in range(nr) for move in alone.get(a, turn[a % 4])])
     else:
-        got = [jnp.zeros_like(message)] * 2
-        for panel in range(2):
-            for k in range(nc):
+        kept = [[], []]
+        for k in range(nc):
+            for panel in range(2):
                 if k != panel:
-                    came = send(message, [((a, panel), (a, k)) for a in range(nr)])
-                    slot = panel if k == 0 else 1 - panel if k > 1 else 0
-                    got[slot] = jnp.where(c == k, came, got[slot])
-    factors, *got = lax.optimization_barrier((factors, *got))
+                    kept[panel if k == 0 else 1 - panel if k > 1 else 0].append((k, panel))
+        for slot in range(2):
+            value = jnp.zeros_like(message)
+            for k, panel in kept[slot]:
+                came = send(message, [((a, panel), (a, k)) for a in range(nr)])
+                value = jnp.where(c == k, came, value)
+                for a in range(nr):
+                    holds[a, k, panel] = slot + 1
+            blocks.append(value)
+    factors, blocks[0], blocks[1] = lax.optimization_barrier((factors, *blocks[:2]))
 
     ratio = nr // nc
 
     parity = [(a, e) for a in range(nr) for e in range(nc) if a % 2 == e % 2]
 
-    def spread(x):
+    def spread_start(x):
         if (nr, nc) == (8, 4):
-            got = send(x, [((e + 4 * g, e), ((e + 4 * g) ^ 2, e)) for e in range(nc) for g in range(2)])
-            side = jnp.where(u == c, x, got)
-            return [side, send(side, [((a, e), (a ^ 4, e)) for a, e in parity])]
+            return [x, send(x, [((e + 4 * g, e), ((e + 4 * g) ^ 2, e)) for e in range(nc) for g in range(2)])]
         near = [x]
         for mask in range(2, nr, 2):
             pairs = [((e + nc * g, e), ((e + nc * g) ^ mask, e)) for e in range(nc) for g in range(ratio)]
             near.append(send(x, pairs))
+        return near
+
+    def spread_end(near):
+        if (nr, nc) == (8, 4):
+            side = jnp.where(u == c, *near)
+            return [side, send(side, [((a, e), (a ^ 4, e)) for a, e in parity])]
         return [choose(near, (r ^ (c + nc * g)) // 2) for g in range(ratio)]
 
-    early = spread(jnp.where(c == 0, message, got[0]))
-    late = spread(jnp.where(c == 0, got[0], jnp.where(c == 1, message, got[1])))
+    near = spread_start(jnp.where(c == 0, blocks[0], blocks[1]))
+    blocks[2], _ = lax.optimization_barrier((blocks[2], near[1]))
+    early = spread_end(near)
+    late = spread_end(spread_start(jnp.where(c == 0, blocks[1], jnp.where(c == 1, blocks[0], blocks[2]))))
     if nc == 4:
-        swap = (u == 0) == (c >= 2)
-        m0 = jnp.where(c == 0, message, jnp.where(swap, got[0], got[1]))
-        m0 = jnp.where(c == 1, jnp.where(u == 0, got[1], got[0]), m0)
-        m1 = jnp.where(c == 1, message, jnp.where(swap, got[1], got[0]))
-        m1 = jnp.where(c == 0, jnp.where(u == 0, got[0], got[1]), m1)
-        mine = jnp.stack([m0, m1])
-        relayed = send(mine, [((a, 3), (a, 2)) if a % 2 else ((a, 2), (a, 3)) for a in range(nr)])
-    else:
-        m0 = jnp.where(c == 0, message, jnp.where(c == 1, got[0], got[1]))
-        mine = jnp.stack([m0, jnp.where(c == 1, message, got[0])])
-        relayed = mine
+        moves = [(0, 0, 1, 0), (0, 2, 3, 2), (0, 3, 2, 2), (1, 1, 0, 0), (1, 2, 3, 2), (1, 3, 2, 2)]
+        relays = [(a, 3, 2) if a % 2 else (a, 2, 3) for a in range(2, nr)]
+        send_round(blocks[1], [(*move, 1) for move in relays])
+        send_round(jnp.where(c < 2, blocks[0], blocks[2]), moves + [(*move, 2) for move in relays])
 
     cols = [jnp.stack([early[g], late[g]]) for g in range(ratio)]
     cols_other = [send(x, [((a, e), (a ^ 1, e)) for a, e in parity]) for x in cols]
     factors_other = send(factors, [((a ^ 1, e), (a, e)) for a, e in parity])
     packed = pltpu.with_memory_space_constraint(packed, pltpu.HBM)
-    arrays = (factors, factors_other, *cols, *cols_other, mine, relayed)
-    return update(tile_scales, packed, arrays, nr, nc, tpr, tpc, n)
+    table = np.array([holds[a, b, p] for a in range(nr) for b in range(nc) for p in range(2)], np.int32)
+    return update(table, tile_scales, packed, (factors, factors_other, *cols, *cols_other), blocks, nr, nc, tpr, tpc, n)
 
 
 def solution(mesh):

time: 75.6 us -> 81 us (1.071)
  the two profiles are of different devices: /device:TPU:24 before, /device:TPU:21 now
where the time goes in v1:
time: 81 us; the launch traced here: 79.4 us
  starting transfers between devices  35.1 us (43%)
  Pallas kernels  25.3 us (31%)
  waiting for transfers between devices  16.7 us (21%)
  other arithmetic  1.18 us (1%)
    ppermute x18, starting transfers between devices, send(): return lax.ppermute(x, ('prow', 'pcol'), table)  35.1 us
    ppermute x18, waiting for transfers between devices, send(): return lax.ppermute(x, ('prow', 'pcol'), table)  16.7 us
    pallas_call x1, Pallas kernels, factor_call(): pl.pallas_call(kernel, out_shape=outs, in_specs=specs or [VMEM] * len(arg...  14.9 us
    pallas_call x1, Pallas kernels, update(): pl.pallas_call(functools.partial(update_kernel, geometry), out_shape=jax....  8.72 us
    pallas_call x1, Pallas kernels, on_device(): pl.pallas_call(pack_kernel, out_shape=(jax.ShapeDtypeStruct((tpr * n + EX...  1.66 us
  transfers between devices with their start and end apart: 18, of which 4 were waited for; matrix products, arithmetic and copies ran while one was open for 0% of the time, Pallas kernels for 19%

profile of v1, /device:TPU:21, one launch (start us, length us, event | category | flops | bytes accessed | tf_op | source)
XLA Modules:
  0.0 79.4 jit_solution(1136692009275749949)
XLA Ops:
  0.0 0.7 copy-done
  0.7 1.7 %pack_panel.1 = (bf16[784,256]{1,0:T(8,128)(2,1)S(1)}, bf16[272,256]{1,0:T(8,128)(2,1)S(1)}) custom-call(f32[3,6]{1,0:T(4,128)S(1)} %copy-done, bf16[768,1536]{1,0:T(8,128)(2,1)} %packed.3), custom_call_target="tpu_custom_call" | custom-call | tf_op jit(solution)/shard_map/pack_panel/pallas_call | solution.py:355
  2.4 0.7 collective-permute-start.3
  3.0 0.7 collective-permute-start.2
  3.7 1.3 %collective-permute-start.1 = (bf16[272,256]{1,0:T(8,128)(2,1)S(1)}, bf16[272,256]{1,0:T(8,128)(2,1)S(1)}, u32[]{:S(2)}, u32[]{:S(2)}) collective-permute-start(bf16[272,256]{1,0:T(8,128)(2,1)S(1)} %get-tuple-element.11), channel_id=1, source_target_pairs={{0,6},{4,14},{5,22}} | collective-permute-start | bytes 417800 | tf_op jit(solution)/shard_map/ppermute | solution.py:353
  5.0 0.7 collective-permute-start
  5.7 0.7 collective-permute-start.7
  6.4 0.0 collective-permute-done.3
  6.4 0.0 collective-permute-done.2
  6.4 4.2 %collective-permute-done.1 = bf16[272,256]{1,0:T(8,128)(2,1)S(1)} collective-permute-done((bf16[272,256]{1,0:T(8,128)(2,1)S(1)}, bf16[272,256]{1,0:T(8,128)(2,1)S(1)}, u32[]{:S(2)}, u32[]{:S(2)}) %collective-permute-start.1) | collective-permute-done | bytes 139296 | tf_op jit(solution)/shard_map/ppermute | solution.py:353
  10.6 0.0 collective-permute-done
  10.6 7.1 %collective-permute-start.6 = (bf16[272,256]{1,0:T(8,128)(2,1)S(1)}, bf16[272,256]{1,0:T(8,128)(2,1)S(1)}, u32[]{:S(2)}, u32[]{:S(2)}) collective-permute-start(bf16[272,256]{1,0:T(8,128)(2,1)S(1)} %select_select_fusion.1.refs_0_), channel_id=1, source_target_pairs={{4,28},{1,25},{6,30},{3,27},{12,20},{9,17},{14,22},{11,19},{20,12}... | collective-permute-start | bytes 417800 | tf_op jit(solution)/shard_map/ppermute | solution.py:353
  17.8 1.9 %collective-permute-start.5 = (bf16[272,256]{1,0:T(8,128)(2,1)S(1)}, bf16[272,256]{1,0:T(8,128)(2,1)S(1)}, u32[]{:S(2)}, u32[]{:S(2)}) collective-permute-start(bf16[272,256]{1,0:T(8,128)(2,1)S(1)} %select_select_fusion.1.refs_0_), channel_id=1, source_target_pairs={{4,20},{1,17},{6,22},{3,19},{12,28},{9,25},{14,30},{11,27},{20,4},... | collective-permute-start | bytes 417800 | tf_op jit(solution)/shard_map/ppermute | solution.py:353
  19.7 1.3 %collective-permute-start.4 = (bf16[272,256]{1,0:T(8,128)(2,1)S(1)}, bf16[272,256]{1,0:T(8,128)(2,1)S(1)}, u32[]{:S(2)}, u32[]{:S(2)}) collective-permute-start(bf16[272,256]{1,0:T(8,128)(2,1)S(1)} %select_select_fusion.1.refs_0_), channel_id=1, source_target_pairs={{4,12},{1,9},{6,14},{3,11},{12,4},{9,1},{14,6},{11,3},{20,28},{17,... | collective-permute-start | bytes 417800 | tf_op jit(solution)/shard_map/ppermute | solution.py:353
  21.0 0.7 collective-permute-start.10
  21.7 0.0 collective-permute-done.6.refs_3_
  21.7 2.2 %collective-permute-done.5.refs_2_ = bf16[272,256]{1,0:T(8,128)(2,1)S(1)} collective-permute-done((bf16[272,256]{1,0:T(8,128)(2,1)S(1)}, bf16[272,256]{1,0:T(8,128)(2,1)S(1)}, u32[]{:S(2)}, u32[]{:S(2)}) %collective-permute-start.5) | collective-permute-done | bytes 139296 | tf_op jit(solution)/shard_map/ppermute | solution.py:353
  23.9 0.0 collective-permute-done.4.refs_1_
  23.9 14.9 %factor_pivots.1.factors = bf16[16,128,128]{2,1,0:T(8,128)(2,1)S(1)} custom-call(bf16[272,256]{1,0:T(8,128)(2,1)S(1)} %select_select_fusion.1.refs_0_, bf16[272,256]{1,0:T(8,128)(2,1)S(1)} %collective-permute-done.4.refs_1_, bf16[272,256]{1,0:T(8,128)(2,1)S(1)} %collective-permute-done.5.refs_2_, bf16[272,256]{1,0:T(8,128)(2,1)S(1)} %collective-permute-done.6.refs_3_), custom_call_target="tpu_custom_call" | custom-call | tf_op jit(solution)/shard_map/factor_pivots/pallas_call | solution.py:199
  38.8 0.0 collective-permute-done.7.rest_5_
  38.8 0.1 broadcast_select_fusion.1
  38.8 0.7 collective-permute-start.9
  39.5 0.0 collective-permute-done.10.rest_6_
  39.6 0.0 collective-permute-done.9
  39.6 0.8 %broadcast_select_fusion = (bf16[784,256]{1,0:T(8,128)(2,1)}, bf16[784,256]{1,0:T(8,128)(2,1)S(1)}) fusion(bf16[784,256]{1,0:T(8,128)(2,1)S(1)} %get-tuple-element.14.rest_4_, bf16[784,256]{1,0:T(8,128)(2,1)S(1)} %collective-permute-done.10.rest_6_, pred[]{:T(512)S(6)} %lt.10, bf16[784,256]{1,0:T(8,128)(2,1)S(1)} %collective-permute-done.7.rest_5_, ...), kind=kLoop, calls=%fused_computation.3 | loop fusion | flops 602112 | bytes 2007043 | tf_op jit(solution)/shard_map/jit(_where)/select_n | solution.py:434
  40.4 0.7 collective-permute-start.11
  41.2 0.0 copy-start.3
  41.2 0.0 copy-start.1
  41.2 0.0 copy-start.2
  41.2 0.8 %collective-permute-start.12 = (bf16[784,256]{1,0:T(8,128)(2,1)S(1)}, bf16[784,256]{1,0:T(8,128)(2,1)S(1)}, u32[]{:S(2)}, u32[]{:S(2)}) collective-permute-start(bf16[784,256]{1,0:T(8,128)(2,1)S(1)} %broadcast_select_fusion.3), channel_id=1, source_target_pairs={{0,16},{2,18},{5,21},{7,23},{8,24},{10,26},{13,29},{15,31},{16,0},... | collective-permute-start | bytes 1204232 | tf_op jit(solution)/shard_map/ppermute | solution.py:353
  42.0 0.0 collective-permute-done.11
  42.1 0.7 collective-permute-start.13
  42.8 0.1 pad_maximum_fusion.rest_0_
  42.9 1.3 %collective-permute-start.14 = (bf16[2,784,256]{2,1,0:T(8,128)(2,1)S(1)}, bf16[2,784,256]{2,1,0:T(8,128)(2,1)S(1)}, u32[]{:S(2)}, u32[]{:S(2)}) collective-permute-start(bf16[2,784,256]{2,1,0:T(8,128)(2,1)S(1)} %pad_maximum_fusion.rest_0_), channel_id=1, source_target_pairs={{0,4},{2,6},{5,1},{7,3},{8,12},{10,14},{13,9},{15,11},{16,20},{18,... | collective-permute-start | bytes 2408456 | tf_op jit(solution)/shard_map/ppermute | solution.py:353
  44.2 0.0 collective-permute-done.12
  44.2 0.0 collective-permute-done.13
  44.2 0.1 pad_maximum_fusion.1.rest_1_
  44.3 1.3 %collective-permute-start.15 = (bf16[2,784,256]{2,1,0:T(8,128)(2,1)S(1)}, bf16[2,784,256]{2,1,0:T(8,128)(2,1)S(1)}, u32[]{:S(2)}, u32[]{:S(2)}) collective-permute-start(bf16[2,784,256]{2,1,0:T(8,128)(2,1)S(1)} %pad_maximum_fusion.1.rest_1_), channel_id=1, source_target_pairs={{0,4},{2,6},{5,1},{7,3},{8,12},{10,14},{13,9},{15,11},{16,20},{18,... | collective-permute-start | bytes 2408456 | tf_op jit(solution)/shard_map/ppermute | solution.py:353
  45.6 12.0 %collective-permute-start.8 = (bf16[16,128,128]{2,1,0:T(8,128)(2,1)S(1)}, bf16[16,128,128]{2,1,0:T(8,128)(2,1)S(1)}, u32[]{:S(2)}, u32[]{:S(2)}) collective-permute-start(bf16[16,128,128]{2,1,0:T(8,128)(2,1)S(1)} %factor_pivots.1.factors), channel_id=1, source_target_pairs={{4,0},{6,2},{1,5},{3,7},{12,8},{14,10},{9,13},{11,15},{20,16},{22,... | collective-permute-start | bytes 1572872 | tf_op jit(solution)/shard_map/ppermute | solution.py:353
  57.6 1.3 %collective-permute-start.16 = (bf16[784,256]{1,0:T(8,128)(2,1)S(1)}, bf16[784,256]{1,0:T(8,128)(2,1)S(1)}, u32[]{:S(2)}, u32[]{:S(2)}) collective-permute-start(bf16[784,256]{1,0:T(8,128)(2,1)S(1)} %collective-permute-done.7.rest_5_), channel_id=1, source_target_pairs={{10,11},{15,14},{18,19},{23,22},{26,27},{31,30}} | collective-permute-start | bytes 1204232 | tf_op jit(solution)/shard_map/ppermute | solution.py:353
  58.9 1.3 %collective-permute-start.17 = (bf16[784,256]{1,0:T(8,128)(2,1)S(1)}, bf16[784,256]{1,0:T(8,128)(2,1)S(1)}, u32[]{:S(2)}, u32[]{:S(2)}) collective-permute-start(bf16[784,256]{1,0:T(8,128)(2,1)S(1)} %copy-done.3), channel_id=1, source_target_pairs={{0,1},{2,3},{3,2},{5,4},{6,7},{7,6},{10,11},{15,14},{18,19},{23,22... | collective-permute-start | bytes 1204232 | tf_op jit(solution)/shard_map/ppermute | solution.py:353
  60.2 6.0 %collective-permute-done.16.rest_7_ = bf16[784,256]{1,0:T(8,128)(2,1)S(1)} collective-permute-done((bf16[784,256]{1,0:T(8,128)(2,1)S(1)}, bf16[784,256]{1,0:T(8,128)(2,1)S(1)}, u32[]{:S(2)}, u32[]{:S(2)}) %collective-permute-start.16) | collective-permute-done | bytes 401440 | tf_op jit(solution)/shard_map/ppermute | solution.py:353
  66.2 0.0 collective-permute-done.8.factors_other
  66.2 4.3 %collective-permute-done.17.rest_8_ = bf16[784,256]{1,0:T(8,128)(2,1)S(1)} collective-permute-done((bf16[784,256]{1,0:T(8,128)(2,1)S(1)}, bf16[784,256]{1,0:T(8,128)(2,1)S(1)}, u32[]{:S(2)}, u32[]{:S(2)}) %collective-permute-start.17) | collective-permute-done | bytes 401440 | tf_op jit(solution)/shard_map/ppermute | solution.py:353
  70.5 0.0 collective-permute-done.14.rest_2_
  70.5 0.0 collective-permute-done.15.rest_3_
  70.5 0.0 copy-done.2
  70.5 8.7 %update_tiles.1 = bf16[768,1536]{1,0:T(8,128)(2,1)} custom-call(s32[64]{0:T(128)S(1)} %copy-done.2, f32[3,6]{1,0:T(4,128)S(1)} %copy-done.1, bf16[768,1536]{1,0:T(8,128)(2,1)} %packed.3, bf16[16,128,128]{2,1,0:T(8,128)(2,1)S(1)} %factor_pivots.1.factors, bf16[16,128,128]{2,1,0:T(8,128)(2,1)S(1)} %collective-permute-done.8.factors_other, ...), custom_call_target="tpu_custom_call" | custom-call | flops 4000000000 | bytes 8388608 | tf_op jit(solution)/shard_map/update_tiles/pallas_call | solution.py:319
  (6 shorter events, 0.1 us)
Async XLA Ops:
  0.0 0.7 copy-start
  2.4 4.0 %collective-permute-start.3 = (bf16[272,256]{1,0:T(8,128)(2,1)S(1)}, bf16[272,256]{1,0:T(8,128)(2,1)S(1)}, u32[]{:S(2)}, u32[]{:S(2)}) collective-permute-start(bf16[272,256]{1,0:T(8,128)(2,1)S(1)} %get-tuple-element.11), channel_id=1, source_target_pairs={{0,4},{4,12},{5,20}} | collective-permute-start | bytes 417800 | tf_op jit(solution)/shard_map/ppermute | solution.py:353
  3.0 3.4 %collective-permute-start.2 = (bf16[272,256]{1,0:T(8,128)(2,1)S(1)}, bf16[272,256]{1,0:T(8,128)(2,1)S(1)}, u32[]{:S(2)}, u32[]{:S(2)}) collective-permute-start(bf16[272,256]{1,0:T(8,128)(2,1)S(1)} %get-tuple-element.11), channel_id=1, source_target_pairs={{0,1},{4,9},{5,17}} | collective-permute-start | bytes 417800 | tf_op jit(solution)/shard_map/ppermute | solution.py:353
  3.7 6.9 %collective-permute-start.1 = (bf16[272,256]{1,0:T(8,128)(2,1)S(1)}, bf16[272,256]{1,0:T(8,128)(2,1)S(1)}, u32[]{:S(2)}, u32[]{:S(2)}) collective-permute-start(bf16[272,256]{1,0:T(8,128)(2,1)S(1)} %get-tuple-element.11), channel_id=1, source_target_pairs={{0,6},{4,14},{5,22}} | collective-permute-start | bytes 417800 | tf_op jit(solution)/shard_map/ppermute | solution.py:353
  5.0 5.6 %collective-permute-start = (bf16[272,256]{1,0:T(8,128)(2,1)S(1)}, bf16[272,256]{1,0:T(8,128)(2,1)S(1)}, u32[]{:S(2)}, u32[]{:S(2)}) collective-permute-start(bf16[272,256]{1,0:T(8,128)(2,1)S(1)} %get-tuple-element.11), channel_id=1, source_target_pairs={{0,3},{4,11},{5,19}} | collective-permute-start | bytes 417800 | tf_op jit(solution)/shard_map/ppermute | solution.py:353
  5.7 33.1 %collective-permute-start.7 = (bf16[784,256]{1,0:T(8,128)(2,1)S(1)}, bf16[784,256]{1,0:T(8,128)(2,1)S(1)}, u32[]{:S(2)}, u32[]{:S(2)}) collective-permute-start(bf16[784,256]{1,0:T(8,128)(2,1)S(1)} %get-tuple-element.14.rest_4_), channel_id=1, source_target_pairs={{1,0},{4,5},{9,10},{8,9},{12,15},{13,12},{17,16},{16,18},{20,21},{... | collective-permute-start | bytes 1204232 | tf_op jit(solution)/shard_map/ppermute | solution.py:353
  10.6 11.1 %collective-permute-start.6 = (bf16[272,256]{1,0:T(8,128)(2,1)S(1)}, bf16[272,256]{1,0:T(8,128)(2,1)S(1)}, u32[]{:S(2)}, u32[]{:S(2)}) collective-permute-start(bf16[272,256]{1,0:T(8,128)(2,1)S(1)} %select_select_fusion.1.refs_0_), channel_id=1, source_target_pairs={{4,28},{1,25},{6,30},{3,27},{12,20},{9,17},{14,22},{11,19},{20,12}... | collective-permute-start | bytes 417800 | tf_op jit(solution)/shard_map/ppermute | solution.py:353
  17.8 6.1 %collective-permute-start.5 = (bf16[272,256]{1,0:T(8,128)(2,1)S(1)}, bf16[272,256]{1,0:T(8,128)(2,1)S(1)}, u32[]{:S(2)}, u32[]{:S(2)}) collective-permute-start(bf16[272,256]{1,0:T(8,128)(2,1)S(1)} %select_select_fusion.1.refs_0_), channel_id=1, source_target_pairs={{4,20},{1,17},{6,22},{3,19},{12,28},{9,25},{14,30},{11,27},{20,4},... | collective-permute-start | bytes 417800 | tf_op jit(solution)/shard_map/ppermute | solution.py:353
  19.7 4.2 %collective-permute-start.4 = (bf16[272,256]{1,0:T(8,128)(2,1)S(1)}, bf16[272,256]{1,0:T(8,128)(2,1)S(1)}, u32[]{:S(2)}, u32[]{:S(2)}) collective-permute-start(bf16[272,256]{1,0:T(8,128)(2,1)S(1)} %select_select_fusion.1.refs_0_), channel_id=1, source_target_pairs={{4,12},{1,9},{6,14},{3,11},{12,4},{9,1},{14,6},{11,3},{20,28},{17,... | collective-permute-start | bytes 417800 | tf_op jit(solution)/shard_map/ppermute | solution.py:353
  21.0 18.5 %collective-permute-start.10 = (bf16[784,256]{1,0:T(8,128)(2,1)S(1)}, bf16[784,256]{1,0:T(8,128)(2,1)S(1)}, u32[]{:S(2)}, u32[]{:S(2)}) collective-permute-start(bf16[784,256]{1,0:T(8,128)(2,1)S(1)} %get-tuple-element.14.rest_4_), channel_id=1, source_target_pairs={{0,2},{1,3},{4,7},{5,6},{8,10},{9,8},{13,15},{12,13},{17,18},{16,1... | collective-permute-start | bytes 1204232 | tf_op jit(solution)/shard_map/ppermute | solution.py:353
  38.8 0.7 collective-permute-start.9
  40.4 1.6 %collective-permute-start.11 = (bf16[784,256]{1,0:T(8,128)(2,1)S(1)}, bf16[784,256]{1,0:T(8,128)(2,1)S(1)}, u32[]{:S(2)}, u32[]{:S(2)}) collective-permute-start(bf16[784,256]{1,0:T(8,128)(2,1)S(1)} %get-tuple-element.18), channel_id=1, source_target_pairs={{0,8},{16,24},{5,13},{21,29},{10,2},{26,18},{15,7},{31,23}} | collective-permute-start | bytes 1204232 | tf_op jit(solution)/shard_map/ppermute | solution.py:353
  41.2 17.7 %copy-start.3 = (bf16[784,256]{1,0:T(8,128)(2,1)S(1)}, bf16[784,256]{1,0:T(8,128)(2,1)}, u32[]{:S(2)}) copy-start(bf16[784,256]{1,0:T(8,128)(2,1)} %get-tuple-element.17) | copy-start | bytes 1204228
  41.2 29.3 %copy-start.1 = (f32[3,6]{1,0:T(4,128)S(1)}, f32[3,6]{1,0:T(4,128)}, u32[]{:S(2)}) copy-start(f32[3,6]{1,0:T(4,128)} %scales.3) | copy-start | bytes 220
  41.2 29.3 %copy-start.2 = (s32[64]{0:T(128)S(1)}, s32[64]{0:T(128)}, u32[]{:S(2)}) copy-start(s32[64]{0:T(128)} %constant.30.clone.table) | copy-start | bytes 772
  41.2 3.0 %collective-permute-start.12 = (bf16[784,256]{1,0:T(8,128)(2,1)S(1)}, bf16[784,256]{1,0:T(8,128)(2,1)S(1)}, u32[]{:S(2)}, u32[]{:S(2)}) collective-permute-start(bf16[784,256]{1,0:T(8,128)(2,1)S(1)} %broadcast_select_fusion.3), channel_id=1, source_target_pairs={{0,16},{2,18},{5,21},{7,23},{8,24},{10,26},{13,29},{15,31},{16,0},... | collective-permute-start | bytes 1204232 | tf_op jit(solution)/shard_map/ppermute | solution.py:353
  42.1 2.1 %collective-permute-start.13 = (bf16[784,256]{1,0:T(8,128)(2,1)S(1)}, bf16[784,256]{1,0:T(8,128)(2,1)S(1)}, u32[]{:S(2)}, u32[]{:S(2)}) collective-permute-start(bf16[784,256]{1,0:T(8,128)(2,1)S(1)} %broadcast_select_fusion.2), channel_id=1, source_target_pairs={{0,16},{2,18},{5,21},{7,23},{8,24},{10,26},{13,29},{15,31},{16,0},... | collective-permute-start | bytes 1204232 | tf_op jit(solution)/shard_map/ppermute | solution.py:353
  42.9 27.7 %collective-permute-start.14 = (bf16[2,784,256]{2,1,0:T(8,128)(2,1)S(1)}, bf16[2,784,256]{2,1,0:T(8,128)(2,1)S(1)}, u32[]{:S(2)}, u32[]{:S(2)}) collective-permute-start(bf16[2,784,256]{2,1,0:T(8,128)(2,1)S(1)} %pad_maximum_fusion.rest_0_), channel_id=1, source_target_pairs={{0,4},{2,6},{5,1},{7,3},{8,12},{10,14},{13,9},{15,11},{16,20},{18,... | collective-permute-start | bytes 2408456 | tf_op jit(solution)/shard_map/ppermute | solution.py:353
  44.3 26.2 %collective-permute-start.15 = (bf16[2,784,256]{2,1,0:T(8,128)(2,1)S(1)}, bf16[2,784,256]{2,1,0:T(8,128)(2,1)S(1)}, u32[]{:S(2)}, u32[]{:S(2)}) collective-permute-start(bf16[2,784,256]{2,1,0:T(8,128)(2,1)S(1)} %pad_maximum_fusion.1.rest_1_), channel_id=1, source_target_pairs={{0,4},{2,6},{5,1},{7,3},{8,12},{10,14},{13,9},{15,11},{16,20},{18,... | collective-permute-start | bytes 2408456 | tf_op jit(solution)/shard_map/ppermute | solution.py:353
  45.6 20.6 %collective-permute-start.8 = (bf16[16,128,128]{2,1,0:T(8,128)(2,1)S(1)}, bf16[16,128,128]{2,1,0:T(8,128)(2,1)S(1)}, u32[]{:S(2)}, u32[]{:S(2)}) collective-permute-start(bf16[16,128,128]{2,1,0:T(8,128)(2,1)S(1)} %factor_pivots.1.factors), channel_id=1, source_target_pairs={{4,0},{6,2},{1,5},{3,7},{12,8},{14,10},{9,13},{11,15},{20,16},{22,... | collective-permute-start | bytes 1572872 | tf_op jit(solution)/shard_map/ppermute | solution.py:353
  57.6 8.6 %collective-permute-start.16 = (bf16[784,256]{1,0:T(8,128)(2,1)S(1)}, bf16[784,256]{1,0:T(8,128)(2,1)S(1)}, u32[]{:S(2)}, u32[]{:S(2)}) collective-permute-start(bf16[784,256]{1,0:T(8,128)(2,1)S(1)} %collective-permute-done.7.rest_5_), channel_id=1, source_target_pairs={{10,11},{15,14},{18,19},{23,22},{26,27},{31,30}} | collective-permute-start | bytes 1204232 | tf_op jit(solution)/shard_map/ppermute | solution.py:353
  58.9 11.6 %collective-permute-start.17 = (bf16[784,256]{1,0:T(8,128)(2,1)S(1)}, bf16[784,256]{1,0:T(8,128)(2,1)S(1)}, u32[]{:S(2)}, u32[]{:S(2)}) collective-permute-start(bf16[784,256]{1,0:T(8,128)(2,1)S(1)} %copy-done.3), channel_id=1, source_target_pairs={{0,1},{2,3},{3,2},{5,4},{6,7},{7,6},{10,11},{15,14},{18,19},{23,22... | collective-permute-start | bytes 1204232 | tf_op jit(solution)/shard_map/ppermute | solution.py:353
